TPU v7x, 256 devices: a whole 4x4x8 slice. The times are simulated.
256 devices in a mesh: row: 32 (over y, z), col: 8 (over x, core).
Axes of the slice: x: 4, y: 4, z: 8, core: 2. Of those that a mesh axis runs over, the one named last changes fastest.
Arguments:
- matrix: float32 [16384, 16384], P('row', 'col'), may hold values from -9 to 9
- reflectors: float32 [16384, 512], P('row'), may hold values from -4 to 4
Outputs:
- banded: float32 [16384, 16384], P('row', 'col')
All inputs are finite; a program needn't handle non-finite values.
Results may differ from a plain program's by a relative error of at most 0.0001.
Values sent between devices are 32-bit elements; how exact they have to be, the bound alone decides.
No kernel may reach another device: no remote copies, remote signals or barrier semaphores. Data moves between devices by JAX's collectives and lax.ppermute only.
A program may use at most 64 MiB of HBM per device.

v0:
```python
import jax
import jax.numpy as jnp
from jax import lax
from jax.sharding import PartitionSpec as P

NB = 256


def from_root(value, axis, source):
    kept = jnp.where(lax.axis_index(axis) == source, value, 0).astype(value.dtype)
    return lax.psum(kept, axis)


def precise(left, right):
    return jnp.dot(left, right, precision=lax.Precision.HIGHEST, preferred_element_type=jnp.float32)


def invert_upper(gram_matrix):
    order = gram_matrix.shape[0]
    half_diag = 0.5 * jnp.diagonal(gram_matrix)
    strict = jnp.triu(gram_matrix, 1) / half_diag[:, None]
    identity = jnp.eye(order, dtype=jnp.float32)
    power = -strict
    result = identity + power
    reach = 2
    while reach < order:
        power = precise(power, power)
        result = precise(result, identity + power)
        reach = reach * 2
    return result / half_diag[None, :]


def panel_block(vec_rows):
    blocks_per_col = lax.axis_size("row") // lax.axis_size("col")
    first_root = lax.axis_index("col") * blocks_per_col
    pieces = [from_root(vec_rows, "row", first_root + offset) for offset in range(blocks_per_col)]
    return jnp.concatenate(pieces, 0)


def update_block(corr_rows):
    blocks_per_col = lax.axis_size("row") // lax.axis_size("col")
    first_root = lax.axis_index("col") * blocks_per_col
    pieces = [from_root(corr_rows, "row", first_root + offset) for offset in range(blocks_per_col)]
    return jnp.concatenate(pieces, 0)


def reflect(current, vec_rows, vec_cols):
    products = lax.psum(precise(current, vec_cols), "col")
    gram_matrix, crossed = lax.psum(
        (precise(vec_rows.T, vec_rows), precise(vec_rows.T, products)), "row"
    )
    triangle = invert_upper(gram_matrix)
    applied = precise(products, triangle)
    middle = precise(triangle.T, precise(crossed, triangle))
    correction = applied - 0.5 * precise(vec_rows, middle)
    corr_cols = update_block(correction)
    return current - precise(vec_rows, corr_cols.T) - precise(correction, vec_cols.T)


def per_device(matrix, reflectors):
    rows_block = matrix.shape[0]
    reflector_count = reflectors.shape[1]
    row_offset = lax.axis_index("row") * rows_block
    index_rows = row_offset + lax.broadcasted_iota(jnp.int32, (rows_block, reflector_count), 0)
    pivot_row = lax.broadcasted_iota(jnp.int32, (rows_block, reflector_count), 1) + NB
    vec_rows = jnp.where(
        index_rows < pivot_row,
        jnp.float32(0.0),
        jnp.where(index_rows == pivot_row, jnp.float32(1.0), reflectors),
    )
    vec_cols = panel_block(vec_rows)
    result = matrix
    for panel_index in range(reflector_count // NB):
        start_col = panel_index * NB
        result = reflect(
            result, vec_rows[:, start_col : start_col + NB], vec_cols[:, start_col : start_col + NB]
        )
    return result


def solution(mesh):
    in_specs = (P("row", "col"), P("row", None))
    out_specs = P("row", "col")
    return jax.shard_map(
        per_device, mesh=mesh, in_specs=in_specs, out_specs=out_specs, check_vma=False
    )
```

profile of v0, /device:TPU:2, one launch (start us, length us, event | category | flops | bytes accessed | tf_op | source)
XLA Modules:
  0.0 988.1 jit_solution(1420491645139338723)
XLA Ops:
  6.5 2.4 broadcast_select_fusion
  10.8 168.0 %all-reduce.25.cloned.1.call-done = (f32[512,512]{1,0:T(8,128)}, f32[512,512]{1,0:T(8,128)}, f32[512,512]{1,0:T(8,128)}, f32[512,512]{1,0:T(8,128)}) async-done(((f32[512,512]{1,0:T(8,128)}, f32[512,512]{1,0:T(8,128)}, f32[512,512]{1,0:T(8,128)}, f32[512,512]{1,0:T(8,128)}), (f32[512,512]{1,0:T(8,128)}, f32[512,512]{1,0:T(8,128)}, f32[512,512]{1,0:T(8,128)}, ...) | async-done | bytes 4194320 | tf_op jit(solution)/shard_map/psum | solution.py:11
  180.2 2.0 constant_dynamic-update-slice_fusion.2
  182.4 1.9 copy-done.2
  184.3 7.9 fusion.22
  192.3 1.7 fusion.37
  194.0 59.3 %all-reduce.13.cloned.1.call-done = f32[512,256]{0,1:T(8,128)} async-done(((f32[512,256]{0,1:T(8,128)}), f32[512,256]{0,1:T(8,128)}) %all-reduce.13.cloned.1.call-update) | async-done | bytes 524304 | tf_op jit(solution)/shard_map/psum | solution.py:48
  253.3 2.7 fusion.35
  256.6 149.1 %all-reduce.23.cloned.1.call-done = (f32[256,256]{1,0:T(8,128)}, f32[256,256]{1,0:T(8,128)}) async-done(((f32[256,256]{1,0:T(8,128)}, f32[256,256]{1,0:T(8,128)}), (f32[256,256]{1,0:T(8,128)}, f32[256,256]{1,0:T(8,128)})) %all-reduce.23.cloned.1.call-update) | async-done | bytes 524304 | tf_op jit(solution)/shard_map/psum | solution.py:49
  405.8 2.6 gather_fusion
  418.1 1.9 broadcast_select_fusion.11
  420.2 151.1 %all-reduce.21.cloned.1.call-done = (f32[512,256]{1,0:T(8,128)}, f32[512,256]{1,0:T(8,128)}, f32[512,256]{1,0:T(8,128)}, f32[512,256]{1,0:T(8,128)}) async-done(((f32[512,256]{1,0:T(8,128)}, f32[512,256]{1,0:T(8,128)}, f32[512,256]{1,0:T(8,128)}, f32[512,256]{1,0:T(8,128)}), (f32[512,256]{1,0:T(8,128)}, f32[512,256]{1,0:T(8,128)}, f32[512,256]{1,0:T(8,128)}, ...) | async-done | bytes 2097168 | tf_op jit(solution)/shard_map/psum | solution.py:11
  571.3 5.5 fusion
  576.9 5.5 subtract_subtract_fusion.1
  582.5 2.0 copy-done
  584.5 4.2 fusion.17
  590.5 59.6 %all-reduce.15.cloned.1.call-done = f32[512,256]{1,0:T(8,128)} async-done(((f32[512,256]{1,0:T(8,128)}), f32[512,256]{1,0:T(8,128)}) %all-reduce.15.cloned.1.call-update) | async-done | bytes 524304 | tf_op jit(solution)/shard_map/psum | solution.py:48
  650.1 2.8 fusion.29
  653.2 149.7 %all-reduce.19.cloned.1.call-done = (f32[256,256]{1,0:T(8,128)}, f32[256,256]{1,0:T(8,128)}) async-done(((f32[256,256]{1,0:T(8,128)}, f32[256,256]{1,0:T(8,128)}), (f32[256,256]{1,0:T(8,128)}, f32[256,256]{1,0:T(8,128)})) %all-reduce.19.cloned.1.call-update) | async-done | bytes 524304 | tf_op jit(solution)/shard_map/psum | solution.py:49
  802.8 2.6 gather_fusion.1
  814.7 2.0 broadcast_select_fusion.7
  816.7 151.5 %all-reduce.17.cloned.1.call-done = (f32[512,256]{1,0:T(8,128)}, f32[512,256]{1,0:T(8,128)}, f32[512,256]{1,0:T(8,128)}, f32[512,256]{1,0:T(8,128)}) async-done(((f32[512,256]{1,0:T(8,128)}, f32[512,256]{1,0:T(8,128)}, f32[512,256]{1,0:T(8,128)}, f32[512,256]{1,0:T(8,128)}), (f32[512,256]{1,0:T(8,128)}, f32[512,256]{1,0:T(8,128)}, f32[512,256]{1,0:T(8,128)}, ...) | async-done | bytes 2097168 | tf_op jit(solution)/shard_map/psum | solution.py:11
  968.2 5.8 fusion.8
  974.0 7.0 subtract_subtract_fusion
  (77 shorter events, 25.0 us)
Async XLA Ops:
  6.5 172.2 %all-reduce.25.cloned.1.call-start = ((), (), s32[]{:S(2)}) async-start(), calls=%async_computation.6 | async-start | bytes 8388608 | tf_op jit(solution)/shard_map/psum | solution.py:11
  10.7 242.6 %all-reduce.13.cloned.1.call-start = ((), (), s32[]{:S(2)}) async-start(), calls=%async_computation | async-start | bytes 1048576 | tf_op jit(solution)/shard_map/psum | solution.py:48
  178.7 3.5 copy-start.8
  178.7 3.5 copy-start.7
  178.7 5.6 copy-start.4
  182.4 1.9 copy-start.2
  192.2 213.6 %all-reduce.23.cloned.1.call-start = ((), (), s32[]{:S(2)}) async-start(), calls=%async_computation.5 | async-start | bytes 1048576 | tf_op jit(solution)/shard_map/psum | solution.py:49
  256.0 315.3 %all-reduce.21.cloned.1.call-start = ((), (), s32[]{:S(2)}) async-start(), calls=%async_computation.4 | async-start | bytes 4194304 | tf_op jit(solution)/shard_map/psum | solution.py:11
  412.0 4.0 copy-start.9
  412.8 4.2 copy-start.5
  420.0 230.1 %all-reduce.15.cloned.1.call-start = ((), (), s32[]{:S(2)}) async-start(), calls=%async_computation.1 | async-start | bytes 1048576 | tf_op jit(solution)/shard_map/psum | solution.py:48
  571.3 5.5 copy-start.3
  582.5 2.0 copy-start
  588.7 214.1 %all-reduce.19.cloned.1.call-start = ((), (), s32[]{:S(2)}) async-start(), calls=%async_computation.3 | async-start | bytes 1048576 | tf_op jit(solution)/shard_map/psum | solution.py:49
  652.9 315.3 %all-reduce.17.cloned.1.call-start = ((), (), s32[]{:S(2)}) async-start(), calls=%async_computation.2 | async-start | bytes 4194304 | tf_op jit(solution)/shard_map/psum | solution.py:11
  809.1 4.0 copy-start.10
  809.9 4.2 copy-start.6
  968.2 5.8 copy-start.1
Sparse Core Ops, SparseCore 0:
  11.4 167.3 all-reduce.24
  192.3 60.8 all-reduce.12
  256.7 149.0 all-reduce.22
  420.1 151.1 all-reduce.20
  588.9 61.2 all-reduce.14
  653.8 148.9 all-reduce.18
  816.8 151.3 all-reduce.16
where the time goes:
time: 996 us; the launch traced here: 988 us
  waiting for transfers between devices  888 us (89%)
  matrix products  67.6 us (7%)
  between operations  14.2 us (1%)
  local copies, waits for them, and re-layouts  12.7 us (1%)
    psum x3, waiting for transfers between devices, from_root(): return lax.psum(kept, axis)  471 us
    psum x2, waiting for transfers between devices, reflect(): lax.psum((precise(vec_rows.T, vec_rows), precise(vec_rows.T, products)),...  299 us
    psum x2, waiting for transfers between devices, reflect(): products = lax.psum(precise(current, vec_cols), 'col')  119 us
    dot_general x46, matrix products, precise(): jnp.dot(left, right, precision=lax.Precision.HIGHEST, preferred_element_t...  67.6 us
  transfers between devices with their start and end apart: 7, of which 7 were waited for; matrix products, arithmetic and copies ran while one was open for 0% of the time, Pallas kernels for 0%

commit v1 on v0

v1 whole, which is shorter than its diff:
```python
import jax
import jax.numpy as jnp
import numpy as np
from jax import lax
from jax.experimental import pallas as pl
from jax.experimental.pallas import tpu as pltpu
from jax.sharding import Mesh, PartitionSpec as P

NB = 256
BLOCK = 128
Y = 4
Z = 8
X = 4
CORES = 2
COLS = X * CORES
EVERY = ("y", "z", "x", "core")
ROW = ("y", "z")
COL = ("x", "core")


def product(left, right, contract, precision=lax.Precision.HIGHEST):
    return lax.dot_general(
        left, right, (((contract[0],), (contract[1],)), ((), ())),
        precision=precision, preferred_element_type=jnp.float32,
    )


def precise(left, right):
    return jnp.matmul(left, right, precision=lax.Precision.HIGHEST, preferred_element_type=jnp.float32)


def join_upper(inverse, strict, size):
    pairs = inverse.shape[0] // 2
    off = jnp.stack(
        [strict[(2 * i) * size : (2 * i + 1) * size, (2 * i + 1) * size : (2 * i + 2) * size] for i in range(pairs)]
    )
    first, second = inverse[0::2], inverse[1::2]
    corner = -precise(precise(first, off), second)
    top = jnp.concatenate([first, corner], 2)
    bottom = jnp.concatenate([jnp.zeros_like(corner), second], 2)
    return jnp.concatenate([top, bottom], 1)


def invert_upper(gram_matrix):
    order = gram_matrix.shape[0]
    rows = lax.broadcasted_iota(jnp.int32, (order, order), 0)
    cols = lax.broadcasted_iota(jnp.int32, (order, order), 1)
    diagonal = jnp.where(rows == cols, 0.5 * gram_matrix, 0.0)
    strict = jnp.where(rows < cols, gram_matrix, 0.0) / jnp.sum(diagonal, 1, keepdims=True)
    count = order // BLOCK
    power = -jnp.stack([strict[i * BLOCK : (i + 1) * BLOCK, i * BLOCK : (i + 1) * BLOCK] for i in range(count)])
    identity = jnp.eye(BLOCK, dtype=jnp.float32)[None]
    result = identity + power
    reach = 2
    while reach < BLOCK:
        power = precise(power, power)
        result = precise(result, identity + power)
        reach = reach * 2
    size = BLOCK
    while size < order:
        result = join_upper(result, strict, size)
        size = size * 2
    return result[0] / jnp.sum(diagonal, 0, keepdims=True)


def split(value):
    high = value.astype(jnp.bfloat16)
    return high, (value - high.astype(jnp.float32)).astype(jnp.bfloat16)


def three_pass(left, right, contract):
    dims = (((contract[0],), (contract[1],)), ((), ()))
    dot = lambda a, b: lax.dot_general(a, b, dims, preferred_element_type=jnp.float32)
    return dot(left[0], right[0]) + (dot(left[0], right[1]) + dot(left[1], right[0]))


def accumulate_kernel(left_ref, right_ref, out_ref):
    term = three_pass(split(left_ref[...]), split(right_ref[...]), (1, 0))

    @pl.when(pl.program_id(0) == 0)
    def _():
        out_ref[...] = term

    @pl.when(pl.program_id(0) > 0)
    def _():
        out_ref[...] += term


def long_product(left, right, depth=512):
    rows, steps = left.shape[0], left.shape[1] // depth
    columns = right.shape[1]
    return pl.pallas_call(
        accumulate_kernel,
        grid=(steps,),
        in_specs=[
            pl.BlockSpec((rows, depth), lambda k: (0, k)),
            pl.BlockSpec((depth, columns), lambda k: (k, 0)),
        ],
        out_specs=pl.BlockSpec((rows, columns), lambda k: (0, 0)),
        out_shape=jax.ShapeDtypeStruct((rows, columns), jnp.float32),
        compiler_params=pltpu.CompilerParams(vmem_limit_bytes=40 * 2**20),
        cost_estimate=pl.CostEstimate(
            flops=6 * rows * left.shape[1] * columns, bytes_accessed=4 * (left.size + right.size), transcendentals=0
        ),
    )(left, right)


def subtract_kernel(base_ref, left_ref, right_ref, out_ref, high_ref, low_ref):
    @pl.when(pl.program_id(0) == 0)
    def _():
        high_ref[...], low_ref[...] = split(left_ref[...])

    term = three_pass((high_ref[...], low_ref[...]), split(right_ref[...]), (1, 1))
    out_ref[...] = base_ref[...] - term


def subtract_product(base, left, right, width=256):
    rows, columns = base.shape
    depth = left.shape[1]
    return pl.pallas_call(
        subtract_kernel,
        grid=(columns // width,),
        in_specs=[
            pl.BlockSpec((rows, width), lambda j: (0, j)),
            pl.BlockSpec((rows, depth), lambda j: (0, 0)),
            pl.BlockSpec((width, depth), lambda j: (j, 0)),
        ],
        out_specs=pl.BlockSpec((rows, width), lambda j: (0, j)),
        out_shape=jax.ShapeDtypeStruct((rows, columns), jnp.float32),
        scratch_shapes=[pltpu.VMEM((rows, depth), jnp.bfloat16)] * 2,
        compiler_params=pltpu.CompilerParams(vmem_limit_bytes=40 * 2**20),
        cost_estimate=pl.CostEstimate(
            flops=6 * rows * columns * depth, bytes_accessed=4 * (2 * base.size + right.size), transcendentals=0
        ),
    )(base, left, right)


def exchange(value, axis):
    return lax.all_to_all(value, axis, 0, 0, tiled=True)


def spread(value, axis):
    return exchange(jnp.tile(value, (lax.axis_size(axis),) + (1,) * (value.ndim - 1)), axis)


def sum_pieces(value, count):
    return jnp.sum(value.reshape((count, value.shape[0] // count) + value.shape[1:]), 0)


def all_sum(value, axis):
    count = lax.axis_size(axis)
    piece = sum_pieces(exchange(value.reshape(count * 8, -1), axis), count)
    return spread(piece, axis).reshape(value.shape)


def after(value, other):
    return lax.optimization_barrier((value, other))[0]


TO_COLUMN = [
    (row * COLS + col, ((row % Y) * Z + col) * COLS + row // Y) for row in range(Y * Z) for col in range(COLS)
]


def per_device(matrix, reflectors):
    rows_block, reflector_count = reflectors.shape
    r, c = lax.axis_index(ROW), lax.axis_index(COL)
    index_rows = r * rows_block + lax.broadcasted_iota(jnp.int32, (rows_block, reflector_count), 0)
    pivot_row = lax.broadcasted_iota(jnp.int32, (rows_block, reflector_count), 1) + NB
    vec_rows = jnp.where(
        index_rows < pivot_row,
        jnp.float32(0.0),
        jnp.where(index_rows == pivot_row, jnp.float32(1.0), reflectors),
    )
    piece = rows_block // COLS
    vec_mine = lax.ppermute(lax.dynamic_slice_in_dim(vec_rows, c * piece, piece, 0), EVERY, TO_COLUMN)
    vec_cols = lax.all_gather(vec_mine, ROW, tiled=True)

    width = reflector_count // COLS
    vec_slice = lax.dynamic_slice_in_dim(vec_rows, c * width, width, 1)
    gram_slice = all_sum(after(product(vec_slice, vec_rows, (0, 0)), vec_mine), ROW)
    triangle = invert_upper(spread(gram_slice, COL))
    left_vec = product(vec_rows, triangle, (1, 1))

    vec_cols = after(vec_cols, left_vec)
    part = long_product(matrix, vec_cols)
    prod_piece = sum_pieces(exchange(part, COL), COLS)
    prod_mine = lax.ppermute(prod_piece, EVERY, TO_COLUMN)
    prod_cols = lax.all_gather(prod_mine, ROW, tiled=True)

    prod_rows = spread(after(prod_piece, prod_mine), COL)
    crossed = spread(all_sum(product(vec_slice, prod_rows, (0, 0), lax.Precision.HIGH), ROW), COL)
    crossed = 0.5 * (crossed + crossed.T)
    left_prod = prod_rows - product(left_vec, crossed, (1, 0), lax.Precision.HIGH)
    left_prod = product(left_prod, triangle, (1, 0), lax.Precision.HIGH)
    base = matrix - product(left_prod, vec_cols, (1, 1), lax.Precision.HIGH)
    return subtract_product(base, left_vec, prod_cols)


def solution(mesh):
    torus = Mesh(np.asarray(mesh.devices).reshape(Y, Z, X, CORES), EVERY)
    in_specs = (P(ROW, COL), P(ROW, None))
    out_specs = P(ROW, COL)
    return jax.shard_map(
        per_device, mesh=torus, in_specs=in_specs, out_specs=out_specs, check_vma=False
    )
```

time: 996 us -> 258 us (0.26)
  waiting for transfers between devices: 888 us -> 48.6 us
  blocking collectives: 0 us -> 133 us
  matrix products: 67.6 us -> 17.5 us
  starting transfers between devices: 1.16 us -> 15.5 us
  Pallas kernels: 0 us -> 11.2 us
    psum x7 -> x0, waiting for transfers between devices: 888 us -> none  [the longest x3 471 us: from_root(): return lax.psum(kept, axis)]
    all_to_all x0 -> x7, blocking collectives: none -> 133 us  [exchange(): return lax.all_to_all(value, axis, 0, 0, tiled=True)]
    dot_general x46 -> x22, matrix products: 67.6 us -> 17.5 us  [the longest x6 11.6 us: product(): lax.dot_general(left, right, (((contract[0],), (contract[1],)), ((), ()))...]
    all_gather x0 -> x2, waiting for transfers between devices: none -> 17.3 us  [the longest x1 17.3 us: per_device(): vec_cols = lax.all_gather(vec_mine, ROW, tiled=True)]
    ppermute x0 -> x2, waiting for transfers between devices: none -> 16.8 us  [the longest x1 12.8 us: per_device(): prod_mine = lax.ppermute(prod_piece, EVERY, TO_COLUMN)]
    all_to_all x0 -> x1, waiting for transfers between devices: none -> 14.5 us  [exchange(): return lax.all_to_all(value, axis, 0, 0, tiled=True)]
    pallas_call x0 -> x2, Pallas kernels: none -> 11.2 us  [the longest x1 6.61 us: subtract_product(): pl.pallas_call(subtract_kernel, grid=(columns // width,), in_specs=[pl.Bl...]
  transfers between devices with their start and end apart: 7 -> 5, of which waited for: 7 -> 4; matrix products, arithmetic and copies ran while one was open for 0% -> 8% of each run, Pallas kernels for 0% -> 0%
where the time goes in v1:
time: 258 us; the launch traced here: 256 us
  blocking collectives  133 us (52%)
  waiting for transfers between devices  48.6 us (19%)
  matrix products  17.5 us (7%)
  starting transfers between devices  15.5 us (6%)
  local copies, waits for them, and re-layouts  14.2 us (6%)
  between operations  13.8 us (5%)
  Pallas kernels  11.2 us (4%)
    all_to_all x7, blocking collectives, exchange(): return lax.all_to_all(value, axis, 0, 0, tiled=True)  133 us
    all_gather x1, waiting for transfers between devices, per_device(): vec_cols = lax.all_gather(vec_mine, ROW, tiled=True)  17.3 us
    all_to_all x1, waiting for transfers between devices, exchange(): return lax.all_to_all(value, axis, 0, 0, tiled=True)  14.5 us
    ppermute x1, waiting for transfers between devices, per_device(): prod_mine = lax.ppermute(prod_piece, EVERY, TO_COLUMN)  12.8 us
    dot_general x6, matrix products, product(): lax.dot_general(left, right, (((contract[0],), (contract[1],)), ((), ()))...  11.6 us
    unnamed x24, local copies, waits for them, and re-layouts  11.3 us
    pallas_call x1, Pallas kernels, subtract_product(): pl.pallas_call(subtract_kernel, grid=(columns // width,), in_specs=[pl.Bl...  6.61 us
    all_to_all x1, starting transfers between devices, exchange(): return lax.all_to_all(value, axis, 0, 0, tiled=True)  6.13 us
  transfers between devices with their start and end apart: 5, of which 4 were waited for; matrix products, arithmetic and copies ran while one was open for 8% of the time, Pallas kernels for 0%

profile of v1, /device:TPU:2, one launch (start us, length us, event | category | flops | bytes accessed | tf_op | source)
XLA Modules:
  0.0 256.1 jit_solution(16045861124196186125)
XLA Ops:
  6.5 1.4 select_select_fusion
  8.0 5.2 %collective-permute-start = (f32[64,512]{1,0:T(8,128)S(1)}, f32[64,512]{1,0:T(8,128)S(1)}, u32[]{:S(2)}, u32[]{:S(2)}) collective-permute-start(f32[64,512]{1,0:T(8,128)S(1)} %constant_dynamic-slice_fusion), channel_id=1, source_target_pairs={{0,0},{1,8},{2,16},{3,24},{4,32},{5,40},{6,48},{7,56},{8,64},{9,72... | collective-permute-start | bytes 393224 | tf_op jit(solution)/shard_map/ppermute | solution.py:176
  13.2 4.0 %collective-permute-done = f32[64,512]{1,0:T(8,128)S(1)} collective-permute-done((f32[64,512]{1,0:T(8,128)S(1)}, f32[64,512]{1,0:T(8,128)S(1)}, u32[]{:S(2)}, u32[]{:S(2)}) %collective-permute-start) | collective-permute-done | bytes 131104 | tf_op jit(solution)/shard_map/ppermute | solution.py:176
  18.6 30.5 %all_to_all.66 = f32[32,8,128]{2,1,0:T(8,128)S(1)} all-to-all(f32[32,8,128]{2,1,0:T(8,128)S(1)} %all_to_all.44), channel_id=1, replica_groups=mesh['y'=4,'z'=8,'x'=4,'core'=2] {'y','z'}, dimensions={0} | all-to-all | bytes 262144 | tf_op jit(solution)/shard_map/all_to_all | solution.py:139
  49.2 14.1 %all_to_all.67 = f32[32,8,128]{2,1,0:T(8,128)S(1)} all-to-all(f32[32,8,128]{2,1,0:T(8,128)S(1)} %tile.14), channel_id=1, replica_groups=mesh['y'=4,'z'=8,'x'=4,'core'=2] {'y','z'}, dimensions={0} | all-to-all | bytes 262144 | tf_op jit(solution)/shard_map/all_to_all | solution.py:139
  64.4 6.1 %all-to-all-start.2 = ((f32[8,64,512]{2,1,0:T(8,128)}), f32[8,64,512]{2,1,0:T(8,128)S(1)}, u32[]{:S(2)}, u32[]{:S(2)}) async-start(f32[8,64,512]{2,1,0:T(8,128)} %tile.16), calls=%async_computation.2 | async-start | bytes 2097152 | tf_op jit(solution)/shard_map/all_to_all | solution.py:139
  70.6 14.5 %all-to-all-done.2 = f32[8,64,512]{2,1,0:T(8,128)S(1)} async-done(((f32[8,64,512]{2,1,0:T(8,128)}), f32[8,64,512]{2,1,0:T(8,128)S(1)}, u32[]{:S(2)}, u32[]{:S(2)}) %all-to-all-start.2) | async-done | bytes 1048608 | tf_op jit(solution)/shard_map/all_to_all | solution.py:139
  91.9 1.8 fusion.40.left_ref
  93.7 17.3 %all-gather.3.cloned.1.call-done.right_ref = f32[2048,512]{1,0:T(8,128)} async-done(((f32[64,512]{1,0:T(8,128)}), f32[2048,512]{1,0:T(8,128)}) %all-gather.3.cloned.1.call-update) | async-done | bytes 4194320 | tf_op jit(solution)/shard_map/all_gather | solution.py:177
  111.0 2.2 copy-done.1
  113.2 2.2 copy-done.3
  115.4 4.6 %shard_map.28 = f32[512,512]{1,0:T(8,128)S(1)} custom-call(f32[512,2048]{1,0:T(8,128)S(1)} %copy-done.1, f32[2048,512]{1,0:T(8,128)S(1)} %copy-done.3), custom_call_target="tpu_custom_call" | custom-call | flops 3221225472 | bytes 8388608 | tf_op jit(solution)/shard_map/pallas_call | solution.py:92
  120.1 19.6 %all_to_all.68 = f32[8,64,512]{2,1,0:T(8,128)S(1)} all-to-all(f32[8,64,512]{2,1,0:T(8,128)S(1)} %bitcast.63), channel_id=1, replica_groups=mesh['y'=4,'z'=8,'x'=4,'core'=2] {'x','core'}, dimensions={0} | all-to-all | bytes 2097152 | tf_op jit(solution)/shard_map/all_to_all | solution.py:139
  139.7 4.2 %collective-permute-start.1 = (f32[64,512]{1,0:T(8,128)S(1)}, f32[64,512]{1,0:T(8,128)S(1)}, u32[]{:S(2)}, u32[]{:S(2)}) collective-permute-start(f32[64,512]{1,0:T(8,128)S(1)} %reduce_sum.48), channel_id=1, source_target_pairs={{0,0},{1,8},{2,16},{3,24},{4,32},{5,40},{6,48},{7,56},{8,64},{9,72... | collective-permute-start | bytes 393224 | tf_op jit(solution)/shard_map/ppermute | solution.py:188
  143.9 12.8 %collective-permute-done.1 = f32[64,512]{1,0:T(8,128)S(1)} collective-permute-done((f32[64,512]{1,0:T(8,128)S(1)}, f32[64,512]{1,0:T(8,128)S(1)}, u32[]{:S(2)}, u32[]{:S(2)}) %collective-permute-start.1) | collective-permute-done | bytes 131104 | tf_op jit(solution)/shard_map/ppermute | solution.py:188
  157.4 20.7 %all_to_all.69 = f32[8,64,512]{2,1,0:T(8,128)S(1)} all-to-all(f32[8,64,512]{2,1,0:T(8,128)S(1)} %tile.17), channel_id=1, replica_groups=mesh['y'=4,'z'=8,'x'=4,'core'=2] {'x','core'}, dimensions={0} | all-to-all | bytes 2097152 | tf_op jit(solution)/shard_map/all_to_all | solution.py:139
  178.6 15.7 %all_to_all.70 = f32[32,8,128]{2,1,0:T(8,128)S(1)} all-to-all(f32[32,8,128]{2,1,0:T(8,128)S(1)} %all_to_all.53), channel_id=1, replica_groups=mesh['y'=4,'z'=8,'x'=4,'core'=2] {'y','z'}, dimensions={0} | all-to-all | bytes 262144 | tf_op jit(solution)/shard_map/all_to_all | solution.py:139
  194.4 14.4 %all_to_all.71 = f32[32,8,128]{2,1,0:T(8,128)S(1)} all-to-all(f32[32,8,128]{2,1,0:T(8,128)S(1)} %tile.18), channel_id=1, replica_groups=mesh['y'=4,'z'=8,'x'=4,'core'=2] {'y','z'}, dimensions={0} | all-to-all | bytes 262144 | tf_op jit(solution)/shard_map/all_to_all | solution.py:139
  208.9 18.2 %all_to_all.72 = f32[8,64,512]{2,1,0:T(8,128)S(1)} all-to-all(f32[8,64,512]{2,1,0:T(8,128)S(1)} %tile.20), channel_id=1, replica_groups=mesh['y'=4,'z'=8,'x'=4,'core'=2] {'x','core'}, dimensions={0} | all-to-all | bytes 2097152 | tf_op jit(solution)/shard_map/all_to_all | solution.py:139
  228.4 2.5 convolution_subtract_fusion.1
  233.2 5.0 %convolution_subtract_fusion.base_ref = f32[512,2048]{1,0:T(8,128)} fusion(f32[512,2048]{1,0:T(8,128)S(1)} %copy-done.2, f32[512,512]{1,0:T(8,128)S(1)} %fusion.38, f32[2048,512]{1,0:T(8,128)S(1)} %copy-done.4), kind=kOutput, calls=%fused_computation | convolution fusion | flops 3222274048 | bytes 13631488 | tf_op jit(solution)/shard_map/dot_general | solution.py:22
  238.2 2.2 copy-done
  240.4 2.2 copy-done.5
  242.6 6.6 %shard_map.29 = f32[512,2048]{1,0:T(8,128)} custom-call(f32[512,2048]{1,0:T(8,128)S(1)} %copy-done, f32[512,512]{1,0:T(8,128)S(1)} %fusion.40.left_ref, f32[2048,512]{1,0:T(8,128)S(1)} %copy-done.5), custom_call_target="tpu_custom_call" | custom-call | flops 3221225472 | bytes 12582912 | tf_op jit(solution)/shard_map/pallas_call | solution.py:120
  (68 shorter events, 14.4 us)
Async XLA Ops:
  6.5 104.5 %all-gather.3.cloned.1.call-start = ((), (), s32[]{:S(2)}) async-start(), calls=%async_computation.8 | async-start | bytes 4325376 | tf_op jit(solution)/shard_map/all_gather | solution.py:177
  8.0 9.2 %collective-permute-start = (f32[64,512]{1,0:T(8,128)S(1)}, f32[64,512]{1,0:T(8,128)S(1)}, u32[]{:S(2)}, u32[]{:S(2)}) collective-permute-start(f32[64,512]{1,0:T(8,128)S(1)} %constant_dynamic-slice_fusion), channel_id=1, source_target_pairs={{0,0},{1,8},{2,16},{3,24},{4,32},{5,40},{6,48},{7,56},{8,64},{9,72... | collective-permute-start | bytes 393224 | tf_op jit(solution)/shard_map/ppermute | solution.py:176
  17.2 0.7 copy-start.10
  64.4 20.7 %all-to-all-start.2 = ((f32[8,64,512]{2,1,0:T(8,128)}), f32[8,64,512]{2,1,0:T(8,128)S(1)}, u32[]{:S(2)}, u32[]{:S(2)}) async-start(f32[8,64,512]{2,1,0:T(8,128)} %tile.16), calls=%async_computation.2 | async-start | bytes 2097152 | tf_op jit(solution)/shard_map/all_to_all | solution.py:139
  70.6 167.7 %all-gather.5.cloned.1.call-start = ((), (), s32[]{:S(2)}) async-start(), calls=%async_computation.9 | async-start | bytes 4325376 | tf_op jit(solution)/shard_map/all_gather | solution.py:189
  91.8 28.2 %copy-start.6 = (f32[1,256,256]{2,1,0:T(8,128)}, f32[1,256,256]{2,1,0:T(8,128)S(1)}, u32[]{:S(2)}) copy-start(f32[1,256,256]{2,1,0:T(8,128)S(1)} %get-tuple-element.19) | copy-start | bytes 786436
  91.8 28.2 %copy-start.8 = (f32[1,256,256]{2,1,0:T(8,128)}, f32[1,256,256]{2,1,0:T(8,128)S(1)}, u32[]{:S(2)}) copy-start(f32[1,256,256]{2,1,0:T(8,128)S(1)} %get-tuple-element.20) | copy-start | bytes 786436
  111.0 2.2 copy-start.1
  113.2 2.2 copy-start.3
  139.7 16.9 %collective-permute-start.1 = (f32[64,512]{1,0:T(8,128)S(1)}, f32[64,512]{1,0:T(8,128)S(1)}, u32[]{:S(2)}, u32[]{:S(2)}) collective-permute-start(f32[64,512]{1,0:T(8,128)S(1)} %reduce_sum.48), channel_id=1, source_target_pairs={{0,0},{1,8},{2,16},{3,24},{4,32},{5,40},{6,48},{7,56},{8,64},{9,72... | collective-permute-start | bytes 393224 | tf_op jit(solution)/shard_map/ppermute | solution.py:188
  156.6 0.7 copy-start.11
  228.4 2.5 copy-start.7
  228.4 2.5 copy-start.9
  228.4 3.5 %copy-start.4 = (f32[2048,512]{1,0:T(8,128)S(1)}, f32[2048,512]{1,0:T(8,128)}, u32[]{:S(2)}) copy-start(f32[2048,512]{1,0:T(8,128)} %all-gather.3.cloned.1.call-done.right_ref) | copy-start | bytes 12582916
  230.9 2.3 copy-start.2
  238.2 2.2 copy-start
  240.4 2.2 copy-start.5
Sparse Core Ops, SparseCore 0:
  18.0 93.0 all-gather.2
  157.4 79.3 all-gather.4
